TPU v7x, 128 devices: a whole 4x4x4 slice. The times are simulated.
128 devices in a mesh: freq: 32 (over y, x_lo, z), pair: 4 (over x_hi, core).
Axes of the slice: x: 4 (x_hi: 2, x_lo: 2; x = x_hi * 2 + x_lo), y: 4, z: 4, core: 2. Of those that a mesh axis runs over, the one named last changes fastest.
Arguments:
- vertex: float32 [64, 2, 48, 48, 1024], P('freq', None, None, None, 'pair'), may hold values from -6 to 6
- bubble: float32 [64, 48], P('freq'), may hold values from 0.02 to 0.2
- stencil: float32 [64, 5], P('freq'), may hold values from -3 to 3
- freq_map: int32 [48], replicated, may hold values from 0 to 47
- neighbours: int32 [8192, 3], replicated, may hold values from -1 to 1023, as said below
Outputs:
- section_vertex: float32 [64, 2, 48, 48, 1024], P('freq', None, None, None, 'pair')
Inputs may be any that keep to these rules, and one draw needn't show every extreme that they name: `neighbours`: each pair index 0 to 1023 stands in column 0 of exactly 8 rows; column 1 holds any pair index; column 2 is -1 or 1.
All inputs are finite; a program needn't handle non-finite values.
Results may differ from a plain program's by a relative error of at most 0.0003.
Values sent between devices are 32-bit elements; how exact they have to be, the bound alone decides.
No kernel may reach another device: no remote copies, remote signals or barrier semaphores. Data moves between devices by JAX's collectives and lax.ppermute only.
A program may use at most 320 MiB of HBM per device.

v0:
```python
import functools
import jax
import jax.numpy as jnp
from jax import lax
from jax.experimental import pallas as pl
from jax.experimental.pallas import tpu as pltpu
from jax.sharding import PartitionSpec as P

step_size = 0.25
lanes = 128
sublanes = 8
row_group = 8
main_rows = 34
depth_z = 4
vmem_bytes = 48 * 1024 * 1024


def cost(microseconds):
    return pl.CostEstimate(
        flops=0, bytes_accessed=int(microseconds * 3.0e3), transcendentals=0
    )


def group_of(count):
    return min((8, 6), key=lambda size: -(-count // size) * size)


def contract(left, right, first, rows, write):
    depth = right.shape[0]
    tiles = right.shape[1] // sublanes
    sums = [[None] * tiles for _ in range(rows)]
    for w in range(depth):
        columns = [right[w, sublanes * t : sublanes * (t + 1), :] for t in range(tiles)]
        for i in range(rows):
            row = jnp.broadcast_to(left[first + i, w : w + 1, :], (sublanes, lanes))
            for t in range(tiles):
                term = row * columns[t]
                sums[i][t] = term if w == 0 else sums[i][t] + term
    for i in range(rows):
        for t in range(tiles):
            write(i, t, sums[i][t])


def pack_kernel(rows, vertex, packed):
    def one(u, carry):
        packed[0, u] = vertex[0, 0, rows[u]]
        return carry

    lax.fori_loop(0, packed.shape[1], one, 0)


def pack(vertex, rows, component, half=None):
    slots, _, width, depth, pairs = vertex.shape
    columns = pairs if half is None else lanes
    place = half or 0
    count = rows.shape[0]
    return pl.pallas_call(
        pack_kernel,
        grid_spec=pltpu.PrefetchScalarGridSpec(
            num_scalar_prefetch=1,
            grid=(slots,),
            in_specs=[
                pl.BlockSpec(
                    (1, 1, width, depth, columns), lambda s, r: (s, component, 0, 0, place)
                )
            ],
            out_specs=pl.BlockSpec((1, count, depth, columns), lambda s, r: (s, 0, 0, 0)),
        ),
        out_shape=jax.ShapeDtypeStruct((slots, count, depth, columns), jnp.float32),
        compiler_params=pltpu.CompilerParams(vmem_limit_bytes=vmem_bytes),
        cost_estimate=cost(3),
        name="pack",
    )(rows, vertex)


def lattice_kernel(own, near, far, far_near, coupling, bubble, spin, out, held):
    rows, depth, pairs = held.shape
    total = jnp.zeros((rows * depth, pairs), jnp.float32)
    for j, part in enumerate((own, near, far, far_near)):
        block = part[...].reshape(rows * depth, pairs)
        high = block.astype(jnp.bfloat16)
        low = (block - high.astype(jnp.float32)).astype(jnp.bfloat16)
        matrix = coupling[j]
        total = total + jnp.dot(high, matrix, preferred_element_type=jnp.float32)
        total = total + jnp.dot(low, matrix, preferred_element_type=jnp.float32)
    held[...] = total.reshape(rows, depth, pairs)
    row_0 = pl.program_id(1) * rows
    for half in range(pairs // lanes):
        columns = pl.ds(half * lanes, lanes)
        for i in range(rows):
            held[i, :, columns] = held[i, :, columns] * bubble[0]

        def write(i, t, value, columns=columns):
            tile = pl.ds(sublanes * t, sublanes)
            out[0, 0, i, tile, columns] = spin[0, 0, row_0 + i, tile, columns] - value

        contract(held.at[:, :, columns], spin.at[0, 0, :, :, columns], 0, rows, write)


def lattice(vertex, near, far, far_near, coupling, bubble):
    slots, components, width, depth, pairs = vertex.shape
    part = pl.BlockSpec((None, row_group, depth, pairs), lambda s, j: (s, j, 0, 0))
    return pl.pallas_call(
        lattice_kernel,
        grid=(slots, width // row_group),
        in_specs=[
            pl.BlockSpec((None, None, row_group, depth, pairs), lambda s, j: (s, 0, j, 0, 0)),
            part,
            part,
            part,
            pl.BlockSpec(coupling.shape, lambda s, j: (0, 0, 0)),
            pl.BlockSpec((1, depth, lanes), lambda s, j: (s, 0, 0)),
            pl.BlockSpec((1, 1, width, depth, pairs), lambda s, j: (s, 0, 0, 0, 0)),
        ],
        out_specs=pl.BlockSpec((1, 1, row_group, depth, pairs), lambda s, j: (s, 0, j, 0, 0)),
        out_shape=jax.ShapeDtypeStruct(vertex.shape, jnp.float32),
        scratch_shapes=[pltpu.VMEM((row_group, depth, pairs), jnp.float32)],
        compiler_params=pltpu.CompilerParams(vmem_limit_bytes=vmem_bytes),
        cost_estimate=cost(28),
        name="lattice",
    )(vertex, near, far, far_near, coupling, bubble, vertex)


def crossed_kernel(
    has_relay, has_base, rows, places, stencil, vertex, before, after, bubble, *rest
):
    relay = rest[0]
    base = rest[1 if has_relay else 0]
    out, weighted, result = rest[-3:]
    slot = pl.program_id(0)
    count = before.shape[1]
    size = group_of(count)
    scale = bubble[0]

    if has_relay:
        plane = lax.axis_index("freq") % depth_z

    def side(direct, s, u, end):
        if has_relay:
            return jnp.where(plane == end, relay[s, u], direct[s, u])
        return direct[s, u]

    def weigh(s):
        def one(u, carry):
            row = rows[u]
            sources = (
                side(before, 0, u, 0),
                side(before, 1, u, 0),
                vertex[0, 0, row],
                vertex[1, 0, row],
                side(after, 0, u, depth_z - 1),
                side(after, 1, u, depth_z - 1),
            )
            mixed = stencil[s, 0] * sources[s]
            for k in range(1, 5):
                mixed = mixed + stencil[s, k] * sources[s + k]
            weighted[u] = mixed * scale
            return carry

        lax.fori_loop(0, count, one, 0)

    for s in range(2):
        pl.when(slot == s)(functools.partial(weigh, s))

    current = vertex.at[slot, 0]

    def group(j, carry):
        first = j * size

        def write(i, t, value):
            result[first + i, sublanes * t : sublanes * (t + 1), :] = value

        contract(weighted, current, first, size, write)
        return carry

    lax.fori_loop(0, weighted.shape[0] // size, group, 0)

    def spread(n, carry):
        start = base[0, 0, n] if has_base else current[n]
        place = places[n]
        inside = (place >= 0) & (place < count)
        row = result[jnp.where(inside, place, 0)]
        out[0, 0, n] = start + jnp.where(inside, row, jnp.zeros_like(row))
        return carry

    lax.fori_loop(0, out.shape[2], spread, 0)


def crossed(
    vertex, rows, places, stencil, before, after, bubble, component, half, has_base, base, relay=None
):
    slots, _, width, depth, _ = vertex.shape
    count = rows.shape[0]
    size = group_of(count)
    padded = -(-count // size) * size
    shape = (slots, count, depth, lanes)
    whole = pl.BlockSpec(shape, lambda s, r, q: (0, 0, 0, 0))
    place = half if before.shape[3] > lanes else 0
    beside = pl.BlockSpec(shape, lambda s, r, q: (0, 0, 0, place))
    block = pl.BlockSpec(
        (1, 1, width, depth, lanes), lambda s, r, q: (s, component, 0, 0, half)
    )
    specs = [
        pl.BlockSpec(memory_space=pltpu.SMEM),
        pl.BlockSpec((slots, 1, width, depth, lanes), lambda s, r, q: (0, component, 0, 0, half)),
        beside,
        beside,
        pl.BlockSpec((1, depth, lanes), lambda s, r, q: (s, 0, 0)),
    ]
    operands = [rows, places, stencil, vertex, before, after, bubble]
    if relay is not None:
        specs.append(whole)
        operands.append(relay)
    if base is not None:
        specs.append(block if has_base else pl.BlockSpec(memory_space=pl.ANY))
        operands.append(base)
    return pl.pallas_call(
        functools.partial(crossed_kernel, relay is not None, has_base),
        grid_spec=pltpu.PrefetchScalarGridSpec(
            num_scalar_prefetch=2,
            grid=(slots,),
            in_specs=specs,
            out_specs=block,
            scratch_shapes=[
                pltpu.VMEM((padded, depth, lanes), jnp.float32),
                pltpu.VMEM((padded, depth, lanes), jnp.float32),
            ],
        ),
        out_shape=jax.ShapeDtypeStruct(vertex.shape, jnp.float32),
        input_output_aliases={} if base is None else {len(operands) - 1: 0},
        compiler_params=pltpu.CompilerParams(vmem_limit_bytes=vmem_bytes),
        cost_estimate=cost(10),
        name="crossed",
    )(*operands)


def coupling_matrices(neighbours, pair_count):
    shards = lax.axis_size("pair")
    own = lax.axis_index("pair")
    pair_column = neighbours[:, 0]
    partner_column = neighbours[:, 1]
    sign_column = neighbours[:, 2]
    inner = lax.iota(jnp.int32, pair_count)
    left_ids = jnp.concatenate([(own ^ j) * pair_count + inner for j in range(shards)])
    right_ids = own * pair_count + inner
    partner_hits = (partner_column[:, None] == left_ids[None, :]).astype(jnp.bfloat16)
    pair_hits = jnp.where(
        pair_column[:, None] == right_ids[None, :], sign_column[:, None], 0
    ).astype(jnp.bfloat16)
    signs = lax.dot_general(
        partner_hits, pair_hits, (((0,), (0,)), ((), ())), preferred_element_type=jnp.float32
    )
    return signs.astype(jnp.bfloat16).reshape(shards, pair_count, pair_count)


def section_of(vertex, bubble, stencil, rows, places, more, neighbours):
    slots, components, width, depth, pairs = vertex.shape
    shards = lax.axis_size("pair")
    devices = lax.axis_size("freq")
    last = depth_z - 1
    onward = [(i, i + 1) for i in range(devices - 1)]
    backward = [(j, i) for i, j in onward]
    onward_inside = [(i, j) for i, j in onward if i % depth_z != last]
    backward_inside = [(j, i) for i, j in onward_inside]
    steps = [(i, j) for i, j in onward if i % depth_z == last]
    lend = [(i, i - 1) for i, _ in steps] + [(j, j + 1) for _, j in steps]
    wrap = [(i, i - last) for i, _ in steps] + [(j, j + last) for _, j in steps]
    sideways = [(i - last, j) for i, j in steps] + [(j + last, i) for i, j in steps]
    relay = [(i - 1, j) for i, j in steps] + [(j + 1, i) for i, j in steps]
    across = [(i, i ^ 2) for i in range(shards)]
    beside = [(i, i ^ 1) for i in range(shards)]
    chunks = [(1, 0), (1, 1), (0, 0), (0, 1)]

    every_row, rows = rows, rows[:main_rows]

    def add(section, j, sides, turned=None):
        component, half = chunks[j]
        return crossed(
            vertex, rows, places, stencil, *sides, scaled, component, half,
            component == 0, section, turned,
        )

    def add_more(turn, section):
        first = (turn + 1) * main_rows
        more_rows = lax.dynamic_slice(every_row, (first,), (width - main_rows,))
        for component, half in chunks:
            section = crossed(
                vertex, more_rows, places - first, stencil,
                *halo(pack(vertex, more_rows, component, half)), scaled, component, half,
                True, section,
            )
        return section

    def halo(packed):
        return lax.ppermute(packed, "freq", onward), lax.ppermute(packed, "freq", backward)

    spin = vertex[:, 0]
    scaled = jnp.broadcast_to((step_size * bubble)[:, :, None], (slots, depth, lanes))
    packed = [pack(vertex, rows, component, half) for component, half in chunks]
    density = pack(vertex, rows, 1)
    near = lax.ppermute(spin, "pair", beside)
    stage = (
        lax.ppermute(spin, "pair", across),
        near,
        lax.ppermute(packed[0], "freq", lend),
        lax.ppermute(density, "freq", onward_inside),
        lax.ppermute(density, "freq", backward_inside),
        lax.ppermute(lax.optimization_barrier((packed[1], near))[0], "freq", wrap),
        coupling_matrices(neighbours, pairs),
        *packed[2:],
    )
    far, near, lent, before, behind, wrapped, coupling, *packed = lax.optimization_barrier(stage)
    section = lattice(vertex, near, far, lax.ppermute(far, "pair", beside), coupling, scaled)
    section = add(section, 1, (before, behind), lax.ppermute(wrapped, "freq", sideways))
    stage = (lax.ppermute(lent, "freq", relay), *halo(packed[0]), section, packed[1])
    relayed, *sides_2, section, packed_3 = lax.optimization_barrier(stage)
    sides_3 = halo(packed_3)
    section = add(section, 0, (before, behind), relayed)
    section = add(section, 2, sides_2)
    section = add(section, 3, sides_3)
    return lax.fori_loop(0, more, add_more, section)


def body(vertex, bubble, stencil, freq_map, neighbours):
    width = vertex.shape[2]
    ids = lax.iota(jnp.int32, width)
    picked = freq_map[:, None] == ids[None, :]
    used = jnp.any(picked, axis=0)
    rank = jnp.sum(jnp.where(used[:, None] & (ids[:, None] <= ids[None, :]), 1, 0), axis=0) - 1
    rows = jnp.sum(jnp.where(used[:, None] & (rank[:, None] == ids[None, :]), ids[:, None], 0), axis=0)
    places = jnp.sum(jnp.where(picked, rank[None, :], 0), axis=1)
    count = rank[width - 1] + 1

    more = (count > main_rows).astype(jnp.int32)
    return section_of(vertex, bubble, stencil, rows, places, more, neighbours)


def solution(mesh):
    in_specs = (P("freq", None, None, None, "pair"), P("freq", None), P("freq", None), P(), P())
    out_specs = P("freq", None, None, None, "pair")
    return jax.shard_map(body, mesh=mesh, in_specs=in_specs, out_specs=out_specs, check_vma=False)
```

profile of v0, /device:TPU:24, one launch (start us, length us, event | category | flops | bytes accessed | tf_op | source)
XLA Modules:
  0.0 267.4 jit_solution(11629255594920872147)
XLA Ops:
  0.0 4.9 %slice_bitcast_fusion = f32[2,48,48,256]{3,2,1,0:T(8,128)} fusion(f32[2,2,48,48,256]{4,3,2,1,0:T(8,128)} %vertex.17), kind=kLoop, calls=%fused_computation.7 | loop fusion | bytes 9437184 | tf_op jit(solution)/shard_map/squeeze | solution.py:297
  4.9 3.0 %collective-permute-start.8 = (f32[2,48,48,256]{3,2,1,0:T(8,128)}, f32[2,48,48,256]{3,2,1,0:T(8,128)}, u32[]{:S(2)}, u32[]{:S(2)}) collective-permute-start(f32[2,48,48,256]{3,2,1,0:T(8,128)} %slice_bitcast_fusion), channel_id=1, source_target_pairs={{0,2},{1,3},{2,0},{3,1},{4,6},{5,7},{6,4},{7,5},{8,10},{9,11},{10,... | collective-permute-start | bytes 14155784 | tf_op jit(solution)/shard_map/ppermute | solution.py:303
  8.3 4.5 %pack.10 = f32[2,34,48,256]{3,2,1,0:T(8,128)} custom-call(s32[34]{0:T(128)S(1)} %bitcast.15, f32[2,2,48,48,256]{4,3,2,1,0:T(8,128)} %vertex.17), custom_call_target="tpu_custom_call" | custom-call | bytes 9000 | tf_op jit(solution)/shard_map/pack/pallas_call | solution.py:57
  12.8 4.2 %collective-permute-start.11 = (f32[2,34,48,256]{3,2,1,0:T(8,128)}, f32[2,34,48,256]{3,2,1,0:T(8,128)S(1)}, u32[]{:S(2)}, u32[]{:S(2)}) collective-permute-start(f32[2,34,48,256]{3,2,1,0:T(8,128)} %pack.10), channel_id=1, source_target_pairs={{0,4},{4,8},{8,12},{16,20},{20,24},{24,28},{32,36},{36,40},{40,44}... | collective-permute-start | bytes 10027016 | tf_op jit(solution)/shard_map/ppermute | solution.py:306
  17.0 1.3 collective-permute-start.12
  18.3 3.4 %pack.11 = f32[2,34,48,128]{3,2,1,0:T(8,128)} custom-call(s32[34]{0:T(128)S(1)} %bitcast.16, f32[2,2,48,48,256]{4,3,2,1,0:T(8,128)} %vertex.17), custom_call_target="tpu_custom_call" | custom-call | bytes 9000 | tf_op jit(solution)/shard_map/pack/pallas_call | solution.py:57
  21.7 3.6 %pack.9 = f32[2,34,48,128]{3,2,1,0:T(8,128)} custom-call(s32[34]{0:T(128)S(1)} %bitcast.17, f32[2,2,48,48,256]{4,3,2,1,0:T(8,128)} %vertex.17), custom_call_target="tpu_custom_call" | custom-call | bytes 9000 | tf_op jit(solution)/shard_map/pack/pallas_call | solution.py:57
  25.2 5.7 %collective-permute-start.10 = (f32[2,34,48,128]{3,2,1,0:T(8,128)}, f32[2,34,48,128]{3,2,1,0:T(8,128)}, u32[]{:S(2)}, u32[]{:S(2)}) collective-permute-start(f32[2,34,48,128]{3,2,1,0:T(8,128)} %pack.9), channel_id=1, source_target_pairs={{12,8},{28,24},{44,40},{60,56},{76,72},{92,88},{108,104},{16,20},{... | collective-permute-start | bytes 5013512 | tf_op jit(solution)/shard_map/ppermute | solution.py:305
  31.0 2.2 copy-done
  33.1 4.9 %collective-permute-start.13 = (f32[2,34,48,128]{3,2,1,0:T(8,128)}, f32[2,34,48,128]{3,2,1,0:T(8,128)}, u32[]{:S(2)}, u32[]{:S(2)}) collective-permute-start(f32[2,34,48,128]{3,2,1,0:T(8,128)} %pack.11), channel_id=1, source_target_pairs={{12,0},{28,16},{44,32},{60,48},{76,64},{92,80},{108,96},{16,28},{3... | collective-permute-start | bytes 5013512 | tf_op jit(solution)/shard_map/ppermute | solution.py:308
  38.1 2.7 %pack.12 = f32[2,34,48,128]{3,2,1,0:T(8,128)S(1)} custom-call(s32[34]{0:T(128)S(1)} %bitcast.18, f32[2,2,48,48,256]{4,3,2,1,0:T(8,128)} %vertex.17), custom_call_target="tpu_custom_call" | custom-call | bytes 9000 | tf_op jit(solution)/shard_map/pack/pallas_call | solution.py:57
  42.0 2.2 pack.13
  44.3 12.1 %fusion.10 = bf16[1024,256]{1,0:T(8,128)(2,1)S(1)} fusion(s32[8192]{0:T(1024)S(1)} %bitcast.25, s32[256]{0:T(256)S(1)} %get-tuple-element.123, s32[8192]{0:T(1024)S(1)} %bitcast.26, s32[1024]{0:T(1024)S(1)} %pad_add_fusion, s32[8192]{0:T(1024)S(1)} %bitcast.24), kind=kOutput, calls=%fused_computation.12 | convolution fusion | flops 4309909504 | bytes 627712 | tf_op jit(solution)/shard_map/dot_general | solution.py:250
  56.4 68.4 %collective-permute-done.10 = f32[2,34,48,128]{3,2,1,0:T(8,128)} collective-permute-done((f32[2,34,48,128]{3,2,1,0:T(8,128)}, f32[2,34,48,128]{3,2,1,0:T(8,128)}, u32[]{:S(2)}, u32[]{:S(2)}) %collective-permute-start.10) | collective-permute-done | bytes 1671200 | tf_op jit(solution)/shard_map/ppermute | solution.py:305
  124.9 2.5 collective-permute-start.17
  127.4 1.5 collective-permute-start.14
  128.9 10.3 %collective-permute-start.15 = (f32[2,34,48,128]{3,2,1,0:T(8,128)}, f32[2,34,48,128]{3,2,1,0:T(8,128)S(1)}, u32[]{:S(2)}, u32[]{:S(2)}) collective-permute-start(f32[2,34,48,128]{3,2,1,0:T(8,128)} %copy-done.2), channel_id=1, source_target_pairs={{0,4},{4,8},{8,12},{12,16},{16,20},{20,24},{24,28},{28,32},{32,36}... | collective-permute-start | bytes 5013512 | tf_op jit(solution)/shard_map/ppermute | solution.py:295
  139.3 1.9 collective-permute-start.16
  141.2 2.2 copy-done.10
  143.5 2.3 copy-done.1
  145.9 25.2 %lattice.1.rest_1_ = f32[2,2,48,48,256]{4,3,2,1,0:T(8,128)} custom-call(f32[2,2,48,48,256]{4,3,2,1,0:T(8,128)} %vertex.17, f32[2,48,48,256]{3,2,1,0:T(8,128)S(1)} %copy-done.1, f32[2,48,48,256]{3,2,1,0:T(8,128)} %collective-permute-done.8.far, f32[2,48,48,256]{3,2,1,0:T(8,128)} %copy-done.10, bf16[4,256,256]{2,1,0:T(8,128)(2,1)S(1)} %bitcast.10, ...), custom_call_target="tpu_custom_call" | custom-call | bytes 84000 | tf_op jit(solution)/shard_map/lattice/pallas_call | solution.py:103
  171.1 12.5 %crossed.8.rest_1_ = f32[2,2,48,48,256]{4,3,2,1,0:T(8,128)} custom-call(s32[34]{0:T(128)S(1)} %bitcast.20, s32[48]{0:T(128)S(1)} %get-tuple-element.178.places, f32[2,5]{1,0:T(2,128)S(1)} %copy-done.11, f32[2,2,48,48,256]{4,3,2,1,0:T(8,128)} %vertex.17, f32[2,34,48,256]{3,2,1,0:T(8,128)S(1)} %collective-permute-done.11.before, ...), custom_call_target="tpu_custom_call", output_to_operand_aliasing={{}: (8, {})} | custom-call | bytes 30000 | tf_op jit(solution)/shard_map/crossed/pallas_call | solution.py:217
  183.5 1.3 copy-done.3
  184.8 23.4 %collective-permute-done.15.before = f32[2,34,48,128]{3,2,1,0:T(8,128)S(1)} collective-permute-done((f32[2,34,48,128]{3,2,1,0:T(8,128)}, f32[2,34,48,128]{3,2,1,0:T(8,128)S(1)}, u32[]{:S(2)}, u32[]{:S(2)}) %collective-permute-start.15) | collective-permute-done | bytes 1671200 | tf_op jit(solution)/shard_map/ppermute | solution.py:295
  208.2 1.2 copy-done.5
  210.9 1.9 collective-permute-start.19
  212.9 6.9 %collective-permute-start.20 = (f32[2,34,48,128]{3,2,1,0:T(8,128)}, f32[2,34,48,128]{3,2,1,0:T(8,128)}, u32[]{:S(2)}, u32[]{:S(2)}) collective-permute-start(f32[2,34,48,128]{3,2,1,0:T(8,128)} %pack.13), channel_id=1, source_target_pairs={{4,0},{8,4},{12,8},{16,12},{20,16},{24,20},{28,24},{32,28},{36,32}... | collective-permute-start | bytes 5013512 | tf_op jit(solution)/shard_map/ppermute | solution.py:295
  221.2 1.4 copy-done.4
  222.6 12.7 %crossed.9.rest_0_ = f32[2,2,48,48,256]{4,3,2,1,0:T(8,128)} custom-call(s32[34]{0:T(128)S(1)} %bitcast.21, s32[48]{0:T(128)S(1)} %get-tuple-element.178.places, f32[2,5]{1,0:T(2,128)S(1)} %copy-done.11, f32[2,2,48,48,256]{4,3,2,1,0:T(8,128)} %vertex.17, f32[2,34,48,256]{3,2,1,0:T(8,128)S(1)} %collective-permute-done.11.before, ...), custom_call_target="tpu_custom_call", output_to_operand_aliasing={{}: (8, {})} | custom-call | bytes 30000 | tf_op jit(solution)/shard_map/crossed/pallas_call | solution.py:217
  235.4 12.3 %crossed.10.rest_0_ = f32[2,2,48,48,256]{4,3,2,1,0:T(8,128)} custom-call(s32[34]{0:T(128)S(1)} %bitcast.22, s32[48]{0:T(128)S(1)} %get-tuple-element.178.places, f32[2,5]{1,0:T(2,128)S(1)} %copy-done.11, f32[2,2,48,48,256]{4,3,2,1,0:T(8,128)} %vertex.17, f32[2,34,48,128]{3,2,1,0:T(8,128)S(1)} %copy-done.6, ...), custom_call_target="tpu_custom_call", output_to_operand_aliasing={{}: (7, {})} | custom-call | bytes 30000 | tf_op jit(solution)/shard_map/crossed/pallas_call | solution.py:217
  247.6 6.3 %collective-permute-done.19.before = f32[2,34,48,128]{3,2,1,0:T(8,128)} collective-permute-done((f32[2,34,48,128]{3,2,1,0:T(8,128)}, f32[2,34,48,128]{3,2,1,0:T(8,128)}, u32[]{:S(2)}, u32[]{:S(2)}) %collective-permute-start.19) | collective-permute-done | bytes 1671200 | tf_op jit(solution)/shard_map/ppermute | solution.py:295
  255.2 12.2 %crossed.11 = f32[2,2,48,48,256]{4,3,2,1,0:T(8,128)} custom-call(s32[34]{0:T(128)S(1)} %bitcast.23, s32[48]{0:T(128)S(1)} %get-tuple-element.178.places, f32[2,5]{1,0:T(2,128)S(1)} %copy-done.11, f32[2,2,48,48,256]{4,3,2,1,0:T(8,128)S(1)} %bitcast.14, f32[2,34,48,128]{3,2,1,0:T(8,128)} %collective-permute-done.19.before, ...), custom_call_target="tpu_custom_call", output_to_operand_aliasing={{}: (7, {})} | custom-call | bytes 30000 | tf_op jit(solution)/shard_map/crossed/pallas_call | solution.py:217
  (60 shorter events, 5.3 us)
Async XLA Ops:
  0.0 7.9 %copy-start.14 = (s32[48]{0:T(128)S(1)}, s32[48]{0:T(128)}, u32[]{:S(2)}) copy-start(s32[48]{0:T(128)} %param.10) | copy-start | bytes 580
  4.9 26.1 %collective-permute-start.9 = (f32[2,48,48,256]{3,2,1,0:T(8,128)}, f32[2,48,48,256]{3,2,1,0:T(8,128)S(1)}, u32[]{:S(2)}, u32[]{:S(2)}) collective-permute-start(f32[2,48,48,256]{3,2,1,0:T(8,128)} %slice_bitcast_fusion), channel_id=1, source_target_pairs={{0,1},{1,0},{2,3},{3,2},{4,5},{5,4},{6,7},{7,6},{8,9},{9,8},{10,11... | collective-permute-start | bytes 14155784 | tf_op jit(solution)/shard_map/ppermute | solution.py:301
  4.9 120.0 %collective-permute-start.8 = (f32[2,48,48,256]{3,2,1,0:T(8,128)}, f32[2,48,48,256]{3,2,1,0:T(8,128)}, u32[]{:S(2)}, u32[]{:S(2)}) collective-permute-start(f32[2,48,48,256]{3,2,1,0:T(8,128)} %slice_bitcast_fusion), channel_id=1, source_target_pairs={{0,2},{1,3},{2,0},{3,1},{4,6},{5,7},{6,4},{7,5},{8,10},{9,11},{10,... | collective-permute-start | bytes 14155784 | tf_op jit(solution)/shard_map/ppermute | solution.py:303
  12.8 25.2 %copy-start.12 = (s32[8192,3]{0,1:T(4,128)S(1)}, s32[8192,3]{0,1:T(4,128)}, u32[]{:S(2)}) copy-start(s32[8192,3]{0,1:T(4,128)} %param.11) | copy-start | bytes 294916
  12.8 112.0 %collective-permute-start.11 = (f32[2,34,48,256]{3,2,1,0:T(8,128)}, f32[2,34,48,256]{3,2,1,0:T(8,128)S(1)}, u32[]{:S(2)}, u32[]{:S(2)}) collective-permute-start(f32[2,34,48,256]{3,2,1,0:T(8,128)} %pack.10), channel_id=1, source_target_pairs={{0,4},{4,8},{8,12},{16,20},{20,24},{24,28},{32,36},{36,40},{40,44}... | collective-permute-start | bytes 10027016 | tf_op jit(solution)/shard_map/ppermute | solution.py:306
  17.0 107.9 %collective-permute-start.12 = (f32[2,34,48,256]{3,2,1,0:T(8,128)}, f32[2,34,48,256]{3,2,1,0:T(8,128)}, u32[]{:S(2)}, u32[]{:S(2)}) collective-permute-start(f32[2,34,48,256]{3,2,1,0:T(8,128)} %pack.10), channel_id=1, source_target_pairs={{4,0},{8,4},{12,8},{20,16},{24,20},{28,24},{36,32},{40,36},{44,40}... | collective-permute-start | bytes 10027016 | tf_op jit(solution)/shard_map/ppermute | solution.py:307
  21.7 20.4 %slice-start = ((s8[9437184]{0:T(1024)(128)(4,1)}), s8[4194304]{0:T(1024)(128)(4,1)S(1)}, s32[]{:S(2)}) async-start(s8[9437184]{0:T(1024)(128)(4,1)} %bitcast.11), calls=%async_computation | async-start | bytes 8388608
  21.7 20.4 %slice-start.1 = ((s8[9437184]{0:T(1024)(128)(4,1)}), s8[1048576]{0:T(1024)(128)(4,1)S(1)}, s32[]{:S(2)}) async-start(s8[9437184]{0:T(1024)(128)(4,1)} %bitcast.11), calls=%async_computation.1 | async-start | bytes 2097152
  25.2 99.6 %collective-permute-start.10 = (f32[2,34,48,128]{3,2,1,0:T(8,128)}, f32[2,34,48,128]{3,2,1,0:T(8,128)}, u32[]{:S(2)}, u32[]{:S(2)}) collective-permute-start(f32[2,34,48,128]{3,2,1,0:T(8,128)} %pack.9), channel_id=1, source_target_pairs={{12,8},{28,24},{44,40},{60,56},{76,72},{92,88},{108,104},{16,20},{... | collective-permute-start | bytes 5013512 | tf_op jit(solution)/shard_map/ppermute | solution.py:305
  31.0 2.2 copy-start
  33.1 91.7 %collective-permute-start.13 = (f32[2,34,48,128]{3,2,1,0:T(8,128)}, f32[2,34,48,128]{3,2,1,0:T(8,128)}, u32[]{:S(2)}, u32[]{:S(2)}) collective-permute-start(f32[2,34,48,128]{3,2,1,0:T(8,128)} %pack.11), channel_id=1, source_target_pairs={{12,0},{28,16},{44,32},{60,48},{76,64},{92,80},{108,96},{16,28},{3... | collective-permute-start | bytes 5013512 | tf_op jit(solution)/shard_map/ppermute | solution.py:308
  38.1 3.9 %slice-start.2 = ((s8[9437184]{0:T(1024)(128)(4,1)}), s8[4194304]{0:T(1024)(128)(4,1)S(1)}, s32[]{:S(2)}) async-start(s8[9437184]{0:T(1024)(128)(4,1)} %bitcast.11), calls=%async_computation.2 | async-start | bytes 8388608
  44.2 96.9 %copy-start.13 = (f32[2,48]{1,0:T(2,128)S(1)}, f32[2,48]{1,0:T(2,128)}, u32[]{:S(2)}) copy-start(f32[2,48]{1,0:T(2,128)} %param.8) | copy-start | bytes 1156
  124.8 16.4 %collective-permute-start.18 = (f32[2,48,48,256]{3,2,1,0:T(8,128)}, f32[2,48,48,256]{3,2,1,0:T(8,128)S(1)}, u32[]{:S(2)}, u32[]{:S(2)}) collective-permute-start(f32[2,48,48,256]{3,2,1,0:T(8,128)} %collective-permute-done.8.far), channel_id=1, source_target_pairs={{0,1},{1,0},{2,3},{3,2},{4,5},{5,4},{6,7},{7,6},{8,9},{9,8},{10,11... | collective-permute-start | bytes 14155784 | tf_op jit(solution)/shard_map/ppermute | solution.py:313
  124.9 46.1 %collective-permute-start.17 = (f32[2,34,48,128]{3,2,1,0:T(8,128)}, f32[2,34,48,128]{3,2,1,0:T(8,128)S(1)}, u32[]{:S(2)}, u32[]{:S(2)}) collective-permute-start(f32[2,34,48,128]{3,2,1,0:T(8,128)} %collective-permute-done.13), channel_id=1, source_target_pairs={{0,16},{16,32},{32,48},{48,64},{64,80},{80,96},{96,112},{28,12},{4... | collective-permute-start | bytes 5013512 | tf_op jit(solution)/shard_map/ppermute | solution.py:314
  127.4 56.1 %collective-permute-start.14 = (f32[2,34,48,128]{3,2,1,0:T(8,128)}, f32[2,34,48,128]{3,2,1,0:T(8,128)S(1)}, u32[]{:S(2)}, u32[]{:S(2)}) collective-permute-start(f32[2,34,48,128]{3,2,1,0:T(8,128)} %collective-permute-done.10), channel_id=1, source_target_pairs={{8,16},{24,32},{40,48},{56,64},{72,80},{88,96},{104,112},{20,12},{... | collective-permute-start | bytes 5013512 | tf_op jit(solution)/shard_map/ppermute | solution.py:315
  128.9 79.2 %collective-permute-start.15 = (f32[2,34,48,128]{3,2,1,0:T(8,128)}, f32[2,34,48,128]{3,2,1,0:T(8,128)S(1)}, u32[]{:S(2)}, u32[]{:S(2)}) collective-permute-start(f32[2,34,48,128]{3,2,1,0:T(8,128)} %copy-done.2), channel_id=1, source_target_pairs={{0,4},{4,8},{8,12},{12,16},{16,20},{20,24},{24,28},{28,32},{32,36}... | collective-permute-start | bytes 5013512 | tf_op jit(solution)/shard_map/ppermute | solution.py:295
  139.3 70.5 %collective-permute-start.16 = (f32[2,34,48,128]{3,2,1,0:T(8,128)}, f32[2,34,48,128]{3,2,1,0:T(8,128)S(1)}, u32[]{:S(2)}, u32[]{:S(2)}) collective-permute-start(f32[2,34,48,128]{3,2,1,0:T(8,128)} %copy-done.2), channel_id=1, source_target_pairs={{4,0},{8,4},{12,8},{16,12},{20,16},{24,20},{28,24},{32,28},{36,32}... | collective-permute-start | bytes 5013512 | tf_op jit(solution)/shard_map/ppermute | solution.py:295
  141.2 2.2 copy-start.10
  143.5 2.3 copy-start.1
  145.9 25.2 %copy-start.11 = (f32[2,5]{1,0:T(2,128)S(1)}, f32[2,5]{1,0:T(2,128)}, u32[]{:S(2)}) copy-start(f32[2,5]{1,0:T(2,128)} %stencil.7) | copy-start | bytes 124
  183.5 1.3 copy-start.3
  208.2 1.2 copy-start.5
  209.7 1.2 copy-start.7
  210.9 43.0 %collective-permute-start.19 = (f32[2,34,48,128]{3,2,1,0:T(8,128)}, f32[2,34,48,128]{3,2,1,0:T(8,128)}, u32[]{:S(2)}, u32[]{:S(2)}) collective-permute-start(f32[2,34,48,128]{3,2,1,0:T(8,128)} %pack.13), channel_id=1, source_target_pairs={{0,4},{4,8},{8,12},{12,16},{16,20},{20,24},{24,28},{28,32},{32,36}... | collective-permute-start | bytes 5013512 | tf_op jit(solution)/shard_map/ppermute | solution.py:295
  212.9 42.3 %collective-permute-start.20 = (f32[2,34,48,128]{3,2,1,0:T(8,128)}, f32[2,34,48,128]{3,2,1,0:T(8,128)}, u32[]{:S(2)}, u32[]{:S(2)}) collective-permute-start(f32[2,34,48,128]{3,2,1,0:T(8,128)} %pack.13), channel_id=1, source_target_pairs={{4,0},{8,4},{12,8},{16,12},{20,16},{24,20},{28,24},{32,28},{36,32}... | collective-permute-start | bytes 5013512 | tf_op jit(solution)/shard_map/ppermute | solution.py:295
  221.2 1.4 copy-start.4
  222.6 12.8 %copy-start.6 = (f32[2,34,48,128]{3,2,1,0:T(8,128)S(1)}, f32[2,34,48,128]{3,2,1,0:T(8,128)}, u32[]{:S(2)}) copy-start(f32[2,34,48,128]{3,2,1,0:T(8,128)} %copy-done.5) | copy-start | bytes 5013508
  222.6 12.8 %copy-start.8 = (f32[2,34,48,128]{3,2,1,0:T(8,128)S(1)}, f32[2,34,48,128]{3,2,1,0:T(8,128)}, u32[]{:S(2)}) copy-start(f32[2,34,48,128]{3,2,1,0:T(8,128)} %copy-done.7) | copy-start | bytes 5013508
  222.6 32.5 %slice-start.3 = ((s8[9437184]{0:T(1024)(128)(4,1)}), s8[4194304]{0:T(1024)(128)(4,1)S(1)}, s32[]{:S(2)}) async-start(s8[9437184]{0:T(1024)(128)(4,1)} %bitcast.13), calls=%async_computation.3 | async-start | bytes 8388608
  222.6 32.5 %slice-start.4 = ((s8[9437184]{0:T(1024)(128)(4,1)}), s8[1048576]{0:T(1024)(128)(4,1)S(1)}, s32[]{:S(2)}) async-start(s8[9437184]{0:T(1024)(128)(4,1)} %bitcast.13), calls=%async_computation.4 | async-start | bytes 2097152
  235.4 19.8 %slice-start.5 = ((s8[9437184]{0:T(1024)(128)(4,1)}), s8[4194304]{0:T(1024)(128)(4,1)S(1)}, s32[]{:S(2)}) async-start(s8[9437184]{0:T(1024)(128)(4,1)} %bitcast.13), calls=%async_computation.5 | async-start | bytes 8388608
  (1 other events, 1.2 us)
where the time goes:
time: 269 us; the launch traced here: 267 us
  waiting for transfers between devices  99.7 us (37%)
  Pallas kernels  91.2 us (34%)
  starting transfers between devices  44.2 us (16%)
  local copies, waits for them, and re-layouts  18.8 us (7%)
  matrix products  12.1 us (4%)
    ppermute x1, waiting for transfers between devices, section_of(): lax.ppermute(packed[0], 'freq', lend)  68.4 us
    pallas_call x4, Pallas kernels, crossed(): pl.pallas_call(functools.partial(crossed_kernel, relay is not None, has_b...  49.7 us
    ppermute x2, waiting for transfers between devices, halo(): lax.ppermute(packed, 'freq', onward)  29.7 us
    pallas_call x1, Pallas kernels, lattice(): pl.pallas_call(lattice_kernel, grid=(slots, width // row_group), in_specs...  25.2 us
    pallas_call x5, Pallas kernels, pack(): pl.pallas_call(pack_kernel, grid_spec=pltpu.PrefetchScalarGridSpec(num_sc...  16.4 us
    unnamed x40, local copies, waits for them, and re-layouts  13.1 us
    ppermute x2, starting transfers between devices, halo(): lax.ppermute(packed, 'freq', onward)  12.2 us
    dot_general x1, matrix products, coupling_matrices(): lax.dot_general(partner_hits, pair_hits, (((0,), (0,)), ((), ())), prefer...  12.1 us
  transfers between devices with their start and end apart: 13, of which 5 were waited for; matrix products, arithmetic and copies ran while one was open for 5% of the time, Pallas kernels for 30%

commit v1 on v0

--- a/solution.py
+++ b/solution.py
@@ -312,8 +312,9 @@
     far, near, lent, before, behind, wrapped, coupling, *packed = lax.optimization_barrier(stage)
     section = lattice(vertex, near, far, lax.ppermute(far, "pair", beside), coupling, scaled)
     section = add(section, 1, (before, behind), lax.ppermute(wrapped, "freq", sideways))
-    stage = (lax.ppermute(lent, "freq", relay), *halo(packed[0]), section, packed[1])
-    relayed, *sides_2, section, packed_3 = lax.optimization_barrier(stage)
+    sides_2 = halo(packed[0])
+    stage = (lax.ppermute(lent, "freq", relay), section, packed[1])
+    relayed, section, packed_3 = lax.optimization_barrier(stage)
     sides_3 = halo(packed_3)
     section = add(section, 0, (before, behind), relayed)
     section = add(section, 2, sides_2)

time: 269 us -> 259 us (0.963)
  waiting for transfers between devices: 99.7 us -> 92 us
    ppermute x2, waiting for transfers between devices: 29.7 us -> 20.6 us  [halo(): lax.ppermute(packed, 'freq', onward)]
    unnamed x40 -> x32, local copies, waits for them, and re-layouts: 13.1 us -> 10.6 us
  transfers between devices with their start and end apart: 13 -> 13, of which waited for: 5 -> 4; matrix products, arithmetic and copies ran while one was open for 5% -> 5% of each run, Pallas kernels for 30% -> 31%
where the time goes in v1:
time: 259 us; the launch traced here: 258 us
  waiting for transfers between devices  92 us (36%)
  Pallas kernels  91.8 us (35%)
  starting transfers between devices  44.3 us (17%)
  local copies, waits for them, and re-layouts  16.3 us (6%)
  matrix products  12.1 us (5%)
    ppermute x1, waiting for transfers between devices, section_of(): lax.ppermute(packed[0], 'freq', lend)  68.4 us
    pallas_call x4, Pallas kernels, crossed(): pl.pallas_call(functools.partial(crossed_kernel, relay is not None, has_b...  50.4 us
    pallas_call x1, Pallas kernels, lattice(): pl.pallas_call(lattice_kernel, grid=(slots, width // row_group), in_specs...  25.2 us
    ppermute x2, waiting for transfers between devices, halo(): lax.ppermute(packed, 'freq', onward)  20.6 us
    pallas_call x5, Pallas kernels, pack(): pl.pallas_call(pack_kernel, grid_spec=pltpu.PrefetchScalarGridSpec(num_sc...  16.3 us
    ppermute x2, starting transfers between devices, halo(): lax.ppermute(packed, 'freq', onward)  14.2 us
    dot_general x1, matrix products, coupling_matrices(): lax.dot_general(partner_hits, pair_hits, (((0,), (0,)), ((), ())), prefer...  12.1 us
    unnamed x32, local copies, waits for them, and re-layouts  10.6 us
  transfers between devices with their start and end apart: 13, of which 4 were waited for; matrix products, arithmetic and copies ran while one was open for 5% of the time, Pallas kernels for 31%

profile of v1, /device:TPU:24, one launch (start us, length us, event | category | flops | bytes accessed | tf_op | source)
XLA Modules:
  0.0 257.9 jit_solution(13294621294740227764)
XLA Ops:
  0.0 4.9 %slice_bitcast_fusion = f32[2,48,48,256]{3,2,1,0:T(8,128)} fusion(f32[2,2,48,48,256]{4,3,2,1,0:T(8,128)} %vertex.17), kind=kLoop, calls=%fused_computation.7 | loop fusion | bytes 9437184 | tf_op jit(solution)/shard_map/squeeze | solution.py:297
  4.9 3.0 %collective-permute-start.8 = (f32[2,48,48,256]{3,2,1,0:T(8,128)}, f32[2,48,48,256]{3,2,1,0:T(8,128)}, u32[]{:S(2)}, u32[]{:S(2)}) collective-permute-start(f32[2,48,48,256]{3,2,1,0:T(8,128)} %slice_bitcast_fusion), channel_id=1, source_target_pairs={{0,2},{1,3},{2,0},{3,1},{4,6},{5,7},{6,4},{7,5},{8,10},{9,11},{10,... | collective-permute-start | bytes 14155784 | tf_op jit(solution)/shard_map/ppermute | solution.py:303
  8.3 4.5 %pack.10 = f32[2,34,48,256]{3,2,1,0:T(8,128)} custom-call(s32[34]{0:T(128)S(1)} %bitcast.15, f32[2,2,48,48,256]{4,3,2,1,0:T(8,128)} %vertex.17), custom_call_target="tpu_custom_call" | custom-call | bytes 9000 | tf_op jit(solution)/shard_map/pack/pallas_call | solution.py:57
  12.8 4.2 %collective-permute-start.11 = (f32[2,34,48,256]{3,2,1,0:T(8,128)}, f32[2,34,48,256]{3,2,1,0:T(8,128)S(1)}, u32[]{:S(2)}, u32[]{:S(2)}) collective-permute-start(f32[2,34,48,256]{3,2,1,0:T(8,128)} %pack.10), channel_id=1, source_target_pairs={{0,4},{4,8},{8,12},{16,20},{20,24},{24,28},{32,36},{36,40},{40,44}... | collective-permute-start | bytes 10027016 | tf_op jit(solution)/shard_map/ppermute | solution.py:306
  16.9 1.3 collective-permute-start.12
  18.2 3.3 %pack.11 = f32[2,34,48,128]{3,2,1,0:T(8,128)} custom-call(s32[34]{0:T(128)S(1)} %bitcast.16, f32[2,2,48,48,256]{4,3,2,1,0:T(8,128)} %vertex.17), custom_call_target="tpu_custom_call" | custom-call | bytes 9000 | tf_op jit(solution)/shard_map/pack/pallas_call | solution.py:57
  21.6 3.6 %pack.9 = f32[2,34,48,128]{3,2,1,0:T(8,128)} custom-call(s32[34]{0:T(128)S(1)} %bitcast.17, f32[2,2,48,48,256]{4,3,2,1,0:T(8,128)} %vertex.17), custom_call_target="tpu_custom_call" | custom-call | bytes 9000 | tf_op jit(solution)/shard_map/pack/pallas_call | solution.py:57
  25.2 5.8 %collective-permute-start.10 = (f32[2,34,48,128]{3,2,1,0:T(8,128)}, f32[2,34,48,128]{3,2,1,0:T(8,128)}, u32[]{:S(2)}, u32[]{:S(2)}) collective-permute-start(f32[2,34,48,128]{3,2,1,0:T(8,128)} %pack.9), channel_id=1, source_target_pairs={{12,8},{28,24},{44,40},{60,56},{76,72},{92,88},{108,104},{16,20},{... | collective-permute-start | bytes 5013512 | tf_op jit(solution)/shard_map/ppermute | solution.py:305
  31.0 2.2 copy-done
  33.2 4.9 %collective-permute-start.13 = (f32[2,34,48,128]{3,2,1,0:T(8,128)}, f32[2,34,48,128]{3,2,1,0:T(8,128)}, u32[]{:S(2)}, u32[]{:S(2)}) collective-permute-start(f32[2,34,48,128]{3,2,1,0:T(8,128)} %pack.11), channel_id=1, source_target_pairs={{12,0},{28,16},{44,32},{60,48},{76,64},{92,80},{108,96},{16,28},{3... | collective-permute-start | bytes 5013512 | tf_op jit(solution)/shard_map/ppermute | solution.py:308
  38.2 2.7 %pack.12 = f32[2,34,48,128]{3,2,1,0:T(8,128)S(1)} custom-call(s32[34]{0:T(128)S(1)} %bitcast.18, f32[2,2,48,48,256]{4,3,2,1,0:T(8,128)} %vertex.17), custom_call_target="tpu_custom_call" | custom-call | bytes 9000 | tf_op jit(solution)/shard_map/pack/pallas_call | solution.py:57
  42.1 2.2 pack.13
  44.3 12.1 %fusion.10 = bf16[1024,256]{1,0:T(8,128)(2,1)S(1)} fusion(s32[8192]{0:T(1024)S(1)} %bitcast.25, s32[256]{0:T(256)S(1)} %get-tuple-element.119, s32[8192]{0:T(1024)S(1)} %bitcast.26, s32[1024]{0:T(1024)S(1)} %pad_add_fusion, s32[8192]{0:T(1024)S(1)} %bitcast.24), kind=kOutput, calls=%fused_computation.12 | convolution fusion | flops 4309909504 | bytes 627712 | tf_op jit(solution)/shard_map/dot_general | solution.py:250
  56.4 68.4 %collective-permute-done.10 = f32[2,34,48,128]{3,2,1,0:T(8,128)} collective-permute-done((f32[2,34,48,128]{3,2,1,0:T(8,128)}, f32[2,34,48,128]{3,2,1,0:T(8,128)}, u32[]{:S(2)}, u32[]{:S(2)}) %collective-permute-start.10) | collective-permute-done | bytes 1671200 | tf_op jit(solution)/shard_map/ppermute | solution.py:305
  124.9 2.5 collective-permute-start.15
  127.4 1.5 collective-permute-start.14
  128.9 10.3 %collective-permute-start.19 = (f32[2,34,48,128]{3,2,1,0:T(8,128)}, f32[2,34,48,128]{3,2,1,0:T(8,128)}, u32[]{:S(2)}, u32[]{:S(2)}) collective-permute-start(f32[2,34,48,128]{3,2,1,0:T(8,128)} %copy-done.2), channel_id=1, source_target_pairs={{0,4},{4,8},{8,12},{12,16},{16,20},{20,24},{24,28},{28,32},{32,36}... | collective-permute-start | bytes 5013512 | tf_op jit(solution)/shard_map/ppermute | solution.py:295
  139.3 1.9 collective-permute-start.20
  141.2 2.2 copy-done.6
  143.5 2.3 copy-done.1
  145.8 25.2 %lattice.1.rest_1_ = f32[2,2,48,48,256]{4,3,2,1,0:T(8,128)} custom-call(f32[2,2,48,48,256]{4,3,2,1,0:T(8,128)} %vertex.17, f32[2,48,48,256]{3,2,1,0:T(8,128)S(1)} %copy-done.1, f32[2,48,48,256]{3,2,1,0:T(8,128)} %collective-permute-done.8.far, f32[2,48,48,256]{3,2,1,0:T(8,128)} %copy-done.6, bf16[4,256,256]{2,1,0:T(8,128)(2,1)S(1)} %bitcast.10, ...), custom_call_target="tpu_custom_call" | custom-call | bytes 84000 | tf_op jit(solution)/shard_map/lattice/pallas_call | solution.py:103
  171.0 12.5 %crossed.8.rest_1_ = f32[2,2,48,48,256]{4,3,2,1,0:T(8,128)} custom-call(s32[34]{0:T(128)S(1)} %bitcast.20, s32[48]{0:T(128)S(1)} %get-tuple-element.174.places, f32[2,5]{1,0:T(2,128)S(1)} %copy-done.7, f32[2,2,48,48,256]{4,3,2,1,0:T(8,128)} %vertex.17, f32[2,34,48,256]{3,2,1,0:T(8,128)S(1)} %collective-permute-done.11.before, ...), custom_call_target="tpu_custom_call", output_to_operand_aliasing={{}: (8, {})} | custom-call | bytes 30000 | tf_op jit(solution)/shard_map/crossed/pallas_call | solution.py:217
  183.5 1.2 copy-done.3
  184.7 3.9 %collective-permute-start.17 = (f32[2,34,48,128]{3,2,1,0:T(8,128)}, f32[2,34,48,128]{3,2,1,0:T(8,128)}, u32[]{:S(2)}, u32[]{:S(2)}) collective-permute-start(f32[2,34,48,128]{3,2,1,0:T(8,128)} %pack.13), channel_id=1, source_target_pairs={{0,4},{4,8},{8,12},{12,16},{16,20},{20,24},{24,28},{28,32},{32,36}... | collective-permute-start | bytes 5013512 | tf_op jit(solution)/shard_map/ppermute | solution.py:295
  188.6 4.9 %collective-permute-start.18 = (f32[2,34,48,128]{3,2,1,0:T(8,128)}, f32[2,34,48,128]{3,2,1,0:T(8,128)}, u32[]{:S(2)}, u32[]{:S(2)}) collective-permute-start(f32[2,34,48,128]{3,2,1,0:T(8,128)} %pack.13), channel_id=1, source_target_pairs={{4,0},{8,4},{12,8},{16,12},{20,16},{24,20},{28,24},{32,28},{36,32}... | collective-permute-start | bytes 5013512 | tf_op jit(solution)/shard_map/ppermute | solution.py:295
  194.9 1.4 copy-done.4
  196.3 12.7 %crossed.9.rest_0_ = f32[2,2,48,48,256]{4,3,2,1,0:T(8,128)} custom-call(s32[34]{0:T(128)S(1)} %bitcast.21, s32[48]{0:T(128)S(1)} %get-tuple-element.174.places, f32[2,5]{1,0:T(2,128)S(1)} %copy-done.7, f32[2,2,48,48,256]{4,3,2,1,0:T(8,128)} %vertex.17, f32[2,34,48,256]{3,2,1,0:T(8,128)S(1)} %collective-permute-done.11.before, ...), custom_call_target="tpu_custom_call", output_to_operand_aliasing={{}: (8, {})} | custom-call | bytes 30000 | tf_op jit(solution)/shard_map/crossed/pallas_call | solution.py:217
  209.1 1.5 collective-permute-done.20.after
  210.5 13.0 %crossed.10.rest_0_ = f32[2,2,48,48,256]{4,3,2,1,0:T(8,128)} custom-call(s32[34]{0:T(128)S(1)} %bitcast.22, s32[48]{0:T(128)S(1)} %get-tuple-element.174.places, f32[2,5]{1,0:T(2,128)S(1)} %copy-done.7, f32[2,2,48,48,256]{4,3,2,1,0:T(8,128)} %vertex.17, f32[2,34,48,128]{3,2,1,0:T(8,128)} %collective-permute-done.19.before, ...), custom_call_target="tpu_custom_call", output_to_operand_aliasing={{}: (7, {})} | custom-call | bytes 30000 | tf_op jit(solution)/shard_map/crossed/pallas_call | solution.py:217
  223.5 20.6 %collective-permute-done.17.before = f32[2,34,48,128]{3,2,1,0:T(8,128)} collective-permute-done((f32[2,34,48,128]{3,2,1,0:T(8,128)}, f32[2,34,48,128]{3,2,1,0:T(8,128)}, u32[]{:S(2)}, u32[]{:S(2)}) %collective-permute-start.17) | collective-permute-done | bytes 1671200 | tf_op jit(solution)/shard_map/ppermute | solution.py:295
  244.1 1.6 collective-permute-done.18.after
  245.7 12.2 %crossed.11 = f32[2,2,48,48,256]{4,3,2,1,0:T(8,128)} custom-call(s32[34]{0:T(128)S(1)} %bitcast.23, s32[48]{0:T(128)S(1)} %get-tuple-element.174.places, f32[2,5]{1,0:T(2,128)S(1)} %copy-done.7, f32[2,2,48,48,256]{4,3,2,1,0:T(8,128)S(1)} %bitcast.14, f32[2,34,48,128]{3,2,1,0:T(8,128)} %collective-permute-done.17.before, ...), custom_call_target="tpu_custom_call", output_to_operand_aliasing={{}: (7, {})} | custom-call | bytes 30000 | tf_op jit(solution)/shard_map/crossed/pallas_call | solution.py:217
  (52 shorter events, 2.5 us)
Async XLA Ops:
  0.0 7.9 %copy-start.10 = (s32[48]{0:T(128)S(1)}, s32[48]{0:T(128)}, u32[]{:S(2)}) copy-start(s32[48]{0:T(128)} %param.10) | copy-start | bytes 580
  4.9 26.1 %collective-permute-start.9 = (f32[2,48,48,256]{3,2,1,0:T(8,128)}, f32[2,48,48,256]{3,2,1,0:T(8,128)S(1)}, u32[]{:S(2)}, u32[]{:S(2)}) collective-permute-start(f32[2,48,48,256]{3,2,1,0:T(8,128)} %slice_bitcast_fusion), channel_id=1, source_target_pairs={{0,1},{1,0},{2,3},{3,2},{4,5},{5,4},{6,7},{7,6},{8,9},{9,8},{10,11... | collective-permute-start | bytes 14155784 | tf_op jit(solution)/shard_map/ppermute | solution.py:301
  4.9 119.9 %collective-permute-start.8 = (f32[2,48,48,256]{3,2,1,0:T(8,128)}, f32[2,48,48,256]{3,2,1,0:T(8,128)}, u32[]{:S(2)}, u32[]{:S(2)}) collective-permute-start(f32[2,48,48,256]{3,2,1,0:T(8,128)} %slice_bitcast_fusion), channel_id=1, source_target_pairs={{0,2},{1,3},{2,0},{3,1},{4,6},{5,7},{6,4},{7,5},{8,10},{9,11},{10,... | collective-permute-start | bytes 14155784 | tf_op jit(solution)/shard_map/ppermute | solution.py:303
  12.8 25.3 %copy-start.8 = (s32[8192,3]{0,1:T(4,128)S(1)}, s32[8192,3]{0,1:T(4,128)}, u32[]{:S(2)}) copy-start(s32[8192,3]{0,1:T(4,128)} %param.11) | copy-start | bytes 294916
  12.8 112.0 %collective-permute-start.11 = (f32[2,34,48,256]{3,2,1,0:T(8,128)}, f32[2,34,48,256]{3,2,1,0:T(8,128)S(1)}, u32[]{:S(2)}, u32[]{:S(2)}) collective-permute-start(f32[2,34,48,256]{3,2,1,0:T(8,128)} %pack.10), channel_id=1, source_target_pairs={{0,4},{4,8},{8,12},{16,20},{20,24},{24,28},{32,36},{36,40},{40,44}... | collective-permute-start | bytes 10027016 | tf_op jit(solution)/shard_map/ppermute | solution.py:306
  16.9 107.9 %collective-permute-start.12 = (f32[2,34,48,256]{3,2,1,0:T(8,128)}, f32[2,34,48,256]{3,2,1,0:T(8,128)}, u32[]{:S(2)}, u32[]{:S(2)}) collective-permute-start(f32[2,34,48,256]{3,2,1,0:T(8,128)} %pack.10), channel_id=1, source_target_pairs={{4,0},{8,4},{12,8},{20,16},{24,20},{28,24},{36,32},{40,36},{44,40}... | collective-permute-start | bytes 10027016 | tf_op jit(solution)/shard_map/ppermute | solution.py:307
  21.6 20.5 %slice-start = ((s8[9437184]{0:T(1024)(128)(4,1)}), s8[4194304]{0:T(1024)(128)(4,1)S(1)}, s32[]{:S(2)}) async-start(s8[9437184]{0:T(1024)(128)(4,1)} %bitcast.11), calls=%async_computation | async-start | bytes 8388608
  21.6 20.5 %slice-start.1 = ((s8[9437184]{0:T(1024)(128)(4,1)}), s8[1048576]{0:T(1024)(128)(4,1)S(1)}, s32[]{:S(2)}) async-start(s8[9437184]{0:T(1024)(128)(4,1)} %bitcast.11), calls=%async_computation.1 | async-start | bytes 2097152
  25.2 99.6 %collective-permute-start.10 = (f32[2,34,48,128]{3,2,1,0:T(8,128)}, f32[2,34,48,128]{3,2,1,0:T(8,128)}, u32[]{:S(2)}, u32[]{:S(2)}) collective-permute-start(f32[2,34,48,128]{3,2,1,0:T(8,128)} %pack.9), channel_id=1, source_target_pairs={{12,8},{28,24},{44,40},{60,56},{76,72},{92,88},{108,104},{16,20},{... | collective-permute-start | bytes 5013512 | tf_op jit(solution)/shard_map/ppermute | solution.py:305
  31.0 2.2 copy-start
  33.2 91.6 %collective-permute-start.13 = (f32[2,34,48,128]{3,2,1,0:T(8,128)}, f32[2,34,48,128]{3,2,1,0:T(8,128)}, u32[]{:S(2)}, u32[]{:S(2)}) collective-permute-start(f32[2,34,48,128]{3,2,1,0:T(8,128)} %pack.11), channel_id=1, source_target_pairs={{12,0},{28,16},{44,32},{60,48},{76,64},{92,80},{108,96},{16,28},{3... | collective-permute-start | bytes 5013512 | tf_op jit(solution)/shard_map/ppermute | solution.py:308
  38.2 3.9 %slice-start.2 = ((s8[9437184]{0:T(1024)(128)(4,1)}), s8[4194304]{0:T(1024)(128)(4,1)S(1)}, s32[]{:S(2)}) async-start(s8[9437184]{0:T(1024)(128)(4,1)} %bitcast.11), calls=%async_computation.2 | async-start | bytes 8388608
  40.9 1.2 copy-start.2
  44.3 84.6 %copy-start.9 = (f32[2,48]{1,0:T(2,128)S(1)}, f32[2,48]{1,0:T(2,128)}, u32[]{:S(2)}) copy-start(f32[2,48]{1,0:T(2,128)} %param.8) | copy-start | bytes 1156
  124.8 16.4 %collective-permute-start.16 = (f32[2,48,48,256]{3,2,1,0:T(8,128)}, f32[2,48,48,256]{3,2,1,0:T(8,128)S(1)}, u32[]{:S(2)}, u32[]{:S(2)}) collective-permute-start(f32[2,48,48,256]{3,2,1,0:T(8,128)} %collective-permute-done.8.far), channel_id=1, source_target_pairs={{0,1},{1,0},{2,3},{3,2},{4,5},{5,4},{6,7},{7,6},{8,9},{9,8},{10,11... | collective-permute-start | bytes 14155784 | tf_op jit(solution)/shard_map/ppermute | solution.py:313
  124.9 46.1 %collective-permute-start.15 = (f32[2,34,48,128]{3,2,1,0:T(8,128)}, f32[2,34,48,128]{3,2,1,0:T(8,128)S(1)}, u32[]{:S(2)}, u32[]{:S(2)}) collective-permute-start(f32[2,34,48,128]{3,2,1,0:T(8,128)} %collective-permute-done.13), channel_id=1, source_target_pairs={{0,16},{16,32},{32,48},{48,64},{64,80},{80,96},{96,112},{28,12},{4... | collective-permute-start | bytes 5013512 | tf_op jit(solution)/shard_map/ppermute | solution.py:314
  127.4 56.0 %collective-permute-start.14 = (f32[2,34,48,128]{3,2,1,0:T(8,128)}, f32[2,34,48,128]{3,2,1,0:T(8,128)S(1)}, u32[]{:S(2)}, u32[]{:S(2)}) collective-permute-start(f32[2,34,48,128]{3,2,1,0:T(8,128)} %collective-permute-done.10), channel_id=1, source_target_pairs={{8,16},{24,32},{40,48},{56,64},{72,80},{88,96},{104,112},{20,12},{... | collective-permute-start | bytes 5013512 | tf_op jit(solution)/shard_map/ppermute | solution.py:316
  128.9 80.1 %collective-permute-start.19 = (f32[2,34,48,128]{3,2,1,0:T(8,128)}, f32[2,34,48,128]{3,2,1,0:T(8,128)}, u32[]{:S(2)}, u32[]{:S(2)}) collective-permute-start(f32[2,34,48,128]{3,2,1,0:T(8,128)} %copy-done.2), channel_id=1, source_target_pairs={{0,4},{4,8},{8,12},{12,16},{16,20},{20,24},{24,28},{28,32},{32,36}... | collective-permute-start | bytes 5013512 | tf_op jit(solution)/shard_map/ppermute | solution.py:295
  139.3 71.3 %collective-permute-start.20 = (f32[2,34,48,128]{3,2,1,0:T(8,128)}, f32[2,34,48,128]{3,2,1,0:T(8,128)}, u32[]{:S(2)}, u32[]{:S(2)}) collective-permute-start(f32[2,34,48,128]{3,2,1,0:T(8,128)} %copy-done.2), channel_id=1, source_target_pairs={{4,0},{8,4},{12,8},{16,12},{20,16},{24,20},{28,24},{32,28},{36,32}... | collective-permute-start | bytes 5013512 | tf_op jit(solution)/shard_map/ppermute | solution.py:295
  141.2 2.2 copy-start.6
  143.5 2.3 copy-start.1
  145.8 25.2 %copy-start.7 = (f32[2,5]{1,0:T(2,128)S(1)}, f32[2,5]{1,0:T(2,128)}, u32[]{:S(2)}) copy-start(f32[2,5]{1,0:T(2,128)} %stencil.7) | copy-start | bytes 124
  183.5 1.2 copy-start.3
  184.7 59.4 %collective-permute-start.17 = (f32[2,34,48,128]{3,2,1,0:T(8,128)}, f32[2,34,48,128]{3,2,1,0:T(8,128)}, u32[]{:S(2)}, u32[]{:S(2)}) collective-permute-start(f32[2,34,48,128]{3,2,1,0:T(8,128)} %pack.13), channel_id=1, source_target_pairs={{0,4},{4,8},{8,12},{12,16},{16,20},{20,24},{24,28},{28,32},{32,36}... | collective-permute-start | bytes 5013512 | tf_op jit(solution)/shard_map/ppermute | solution.py:295
  188.6 57.0 %collective-permute-start.18 = (f32[2,34,48,128]{3,2,1,0:T(8,128)}, f32[2,34,48,128]{3,2,1,0:T(8,128)}, u32[]{:S(2)}, u32[]{:S(2)}) collective-permute-start(f32[2,34,48,128]{3,2,1,0:T(8,128)} %pack.13), channel_id=1, source_target_pairs={{4,0},{8,4},{12,8},{16,12},{20,16},{24,20},{28,24},{32,28},{36,32}... | collective-permute-start | bytes 5013512 | tf_op jit(solution)/shard_map/ppermute | solution.py:295
  194.9 1.4 copy-start.4
  196.3 49.3 %slice-start.3 = ((s8[9437184]{0:T(1024)(128)(4,1)}), s8[4194304]{0:T(1024)(128)(4,1)S(1)}, s32[]{:S(2)}) async-start(s8[9437184]{0:T(1024)(128)(4,1)} %bitcast.13), calls=%async_computation.3 | async-start | bytes 8388608
  196.3 49.3 %slice-start.4 = ((s8[9437184]{0:T(1024)(128)(4,1)}), s8[4194304]{0:T(1024)(128)(4,1)S(1)}, s32[]{:S(2)}) async-start(s8[9437184]{0:T(1024)(128)(4,1)} %bitcast.13), calls=%async_computation.4 | async-start | bytes 8388608
  209.1 36.6 %slice-start.5 = ((s8[9437184]{0:T(1024)(128)(4,1)}), s8[1048576]{0:T(1024)(128)(4,1)S(1)}, s32[]{:S(2)}) async-start(s8[9437184]{0:T(1024)(128)(4,1)} %bitcast.13), calls=%async_computation.5 | async-start | bytes 2097152
